TPU v7x, 32 devices: a whole 2x2x4 slice. The times are simulated.
32 devices in a mesh: grp: 2 (over y), seq: 4 (over z), head: 4 (over x, core).
Axes of the slice: x: 2, y: 2, z: 4, core: 2. Of those that a mesh axis runs over, the one named last changes fastest.
Arguments:
- queries: bfloat16 [3072, 4096], P(('grp', 'seq'), 'head'), parts along dimension 0, may hold values from -6 to 6
- keys: bfloat16 [3072, 2048], P(('grp', 'seq'), 'head'), parts along dimension 0, may hold values from -6 to 6
- values: bfloat16 [3072, 2048], P(('grp', 'seq'), 'head'), parts along dimension 0, may hold values from -16 to 16
- out_weight: bfloat16 [4096, 5376], P('head'), may hold values from -0.5 to 0.5
Outputs:
- mixed: bfloat16 [3072, 5376], P(('grp', 'seq', 'head')), parts along dimension 0
There are 2 independent parts, one for each index of `grp`. A program takes and returns all parts, laid end to end along the dimension named above; an argument that names none is the same for every part. Nothing has to cross between parts.
All inputs are finite; a program needn't handle non-finite values.
Results may differ from a plain program's by a relative error of at most 0.02.
Values may be sent and summed in bfloat16 or wider, within the bound.
A program may use at most 64 MiB of HBM per device.

v0:
```python
import jax
import jax.numpy as jnp
from jax import lax
from jax.sharding import PartitionSpec as P

QUERY_HEADS = 32
KEY_VALUE_HEADS = 16
HEAD_SIZE = 128


attn_scale = 168.0 ** (-0.5)


def shifted_2(value, axis, steps):
    count = lax.axis_size(axis)
    leading, last = (max(0, -steps), min(count, count - steps))
    return lax.ppermute(value, axis, [(source, source + steps) for source in range(leading, last)])


def on_device(queries, keys, values, out_weight):
    row_count = queries.shape[0]
    kv_local = keys.shape[1] // HEAD_SIZE
    group_width = QUERY_HEADS // KEY_VALUE_HEADS
    seq_count = lax.axis_size("seq")
    seq_place = lax.axis_index("seq")
    reaches = [1 << step_level for step_level in range(seq_count.bit_length() - 1)]
    kv_pair = (keys, values)
    arrived = []
    for distance in reaches:
        arrived.append(shifted_2((kv_pair[0], kv_pair[1]), "seq", distance))
    full_keys = jnp.concatenate([keys] + [received[0] for received in arrived], axis=0)
    full_values = jnp.concatenate([values] + [received[1] for received in arrived], axis=0)
    causal = jnp.arange(row_count)[:, None] >= jnp.arange(row_count)[None, :]
    mask_parts = [causal] + [
        jnp.broadcast_to(seq_place >= distance, (row_count, row_count)) for distance in reaches
    ]
    visible = jnp.concatenate(mask_parts, axis=1)
    query_head_stack = queries.reshape(row_count, kv_local, group_width, HEAD_SIZE)
    key_head_stack = full_keys.reshape(-1, kv_local, HEAD_SIZE)
    value_head_stack = full_values.reshape(-1, kv_local, HEAD_SIZE)
    scores = (
        jnp.einsum(
            "tkgd,skd->kgts", query_head_stack, key_head_stack, preferred_element_type=jnp.float32
        )
        * attn_scale
    )
    masked = jnp.where(visible, scores, -jnp.inf)
    row_max = jnp.max(masked, axis=-1, keepdims=True)
    shifted = jnp.exp(masked - row_max)
    row_sum = jnp.sum(shifted, axis=-1, keepdims=True)
    weights = (shifted / row_sum).astype(jnp.bfloat16)
    attended = jnp.einsum(
        "kgts,skd->tkgd", weights, value_head_stack, preferred_element_type=jnp.float32
    )
    attended = attended.astype(jnp.bfloat16).reshape(row_count, -1)
    return lax.psum_scatter(
        jnp.dot(attended, out_weight, preferred_element_type=jnp.float32).astype(jnp.bfloat16),
        "head",
        scatter_dimension=0,
        tiled=True,
    )


def solution(mesh):
    in_specs = (
        P(("grp", "seq"), "head"),
        P(("grp", "seq"), "head"),
        P(("grp", "seq"), "head"),
        P("head", None),
    )
    out_specs = P(("grp", "seq", "head"), None)
    return jax.shard_map(
        on_device, mesh=mesh, in_specs=in_specs, out_specs=out_specs, check_vma=False
    )
```

profile of v0, /device:TPU:21, one launch (start us, length us, event | category | flops | bytes accessed | tf_op | source)
XLA Modules:
  0.0 142.0 jit_solution(6702208322434794727)
XLA Ops:
  6.5 0.0 copy-start.1
  6.5 0.0 reduce-scatter.2.cloned.1.call-start
  6.5 1.3 copy.11
  7.8 1.3 collective-permute-start.3
  9.1 3.2 %collective-permute-start.2 = (bf16[384,512]{0,1:T(8,128)(2,1)S(1)}, bf16[384,512]{0,1:T(8,128)(2,1)}, u32[]{:S(2)}, u32[]{:S(2)}) collective-permute-start(bf16[384,512]{0,1:T(8,128)(2,1)S(1)} %copy.11), channel_id=1, source_target_pairs={{0,4},{4,8},{8,12},{1,5},{5,9},{9,13},{2,6},{6,10},{10,14},{3,7},{... | collective-permute-start | bytes 1179656 | tf_op jit(solution)/shard_map/ppermute | solution.py:17
  12.3 1.9 %collective-permute-start = (bf16[384,512]{1,0:T(8,128)(2,1)}, bf16[384,512]{1,0:T(8,128)(2,1)S(1)}, u32[]{:S(2)}, u32[]{:S(2)}) collective-permute-start(bf16[384,512]{1,0:T(8,128)(2,1)} %param.6), channel_id=1, source_target_pairs={{0,4},{4,8},{8,12},{1,5},{5,9},{9,13},{2,6},{6,10},{10,14},{3,7},{... | collective-permute-start | bytes 1179656 | tf_op jit(solution)/shard_map/ppermute | solution.py:17
  14.2 1.3 collective-permute-start.1
  15.7 1.8 %add_add_fusion = pred[384,1152]{0,1:T(8,128)(4,1)} fusion(pred[384,384]{0,1:T(8,128)(4,1)S(1)} %iota_compare_fusion, pred[1152]{0:T(1024)(128)(4,1)S(1)} %pad.5.clone, pred[1152]{0:T(1024)(128)(4,1)S(1)} %pad.4.clone), kind=kLoop, calls=%fused_computation.10 | loop fusion | flops 884736 | bytes 592128 | tf_op jit(solution)/shard_map/concatenate | solution.py:37
  17.4 2.6 %reshape.16 = bf16[384,4,2,128]{3,2,1,0:T(2,128)(2,1)S(1)} reshape(bf16[384,1024]{1,0:T(8,128)(2,1)} %param.4) | data formatting | bytes 1572864 | tf_op jit(solution)/shard_map/reshape | solution.py:38
  20.0 0.0 copy-start
  20.0 35.4 %collective-permute-done = bf16[384,512]{1,0:T(8,128)(2,1)S(1)} collective-permute-done((bf16[384,512]{1,0:T(8,128)(2,1)}, bf16[384,512]{1,0:T(8,128)(2,1)S(1)}, u32[]{:S(2)}, u32[]{:S(2)}) %collective-permute-start) | collective-permute-done | bytes 393248 | tf_op jit(solution)/shard_map/ppermute | solution.py:17
  55.4 0.0 collective-permute-done.1
  55.4 0.0 copy-done.1
  55.4 0.1 pad_maximum_fusion
  55.5 0.7 copy.8
  56.2 0.0 collective-permute-done.3
  56.2 0.0 collective-permute-done.2
  56.2 1.2 pad_maximum_fusion.1
  57.4 0.0 copy-done
  57.4 6.2 %fusion.25 = f32[4,2,384]{2,1,0:T(2,128)S(1)} fusion(pred[384,1152]{0,1:T(8,128)(4,1)} %add_add_fusion, bf16[1152,4,128,1]{0,2,3,1:T(8,128)(2,1)S(1)} %bitcast.30, bf16[384,4,2,128]{3,2,1,0:T(2,128)(2,1)S(1)} %reshape.16), kind=kOutput, calls=%fused_computation.23 | convolution fusion | flops 920126592 | bytes 2420736 | tf_op jit(solution)/shard_map/sub | solution.py:49
  63.7 7.8 %fusion.8 = bf16[4,128,2,384]{3,1,2,0:T(8,128)(2,1)S(1)} fusion(bf16[1152,4,128,1]{0,2,3,1:T(8,128)(2,1)S(1)} %bitcast.29, f32[4,2,384]{2,1,0:T(2,128)S(1)} %fusion.25, pred[384,1152]{0,1:T(8,128)(4,1)} %add_add_fusion, bf16[1152,4,128,1]{0,2,3,1:T(8,128)(2,1)S(1)} %bitcast.31, bf16[384,4,2,128]{3,2,1,0:T(2,128)(2,1)} %copy-done), kind=kOutput, calls=%fused_computation.12 | convolution fusion | flops 1830031488 | bytes 4386816 | tf_op jit(solution)/shard_map/kgts,skd->tkgd/dot_general | solution.py:52
  71.5 10.3 %convolution_convert_fusion = bf16[384,5376]{1,0:T(8,128)(2,1)} fusion(bf16[384,1024]{0,1:T(8,128)(2,1)S(1)} %bitcast.32, bf16[1024,5376]{1,0:T(8,128)(2,1)} %param.7), kind=kOutput, calls=%fused_computation.5 | convolution fusion | flops 4229922816 | bytes 15925248 | tf_op jit(solution)/shard_map/dot_general | solution.py:57
  81.8 0.0 reduce-scatter.2.cloned.1.call-update
  81.8 53.4 %reduce-scatter.2.cloned.1.call-done = bf16[96,5376]{1,0:T(8,128)(2,1)} async-done(((bf16[384,5376]{1,0:T(8,128)(2,1)}), bf16[96,5376]{1,0:T(8,128)(2,1)}) %reduce-scatter.2.cloned.1.call-update) | async-done | bytes 1032208 | tf_op jit(solution)/shard_map/reduce_scatter | solution.py:56
  (5 shorter events, 0.1 us)
Async XLA Ops:
  6.5 48.9 %copy-start.1 = (bf16[384,512]{1,0:T(8,128)(2,1)S(1)}, bf16[384,512]{1,0:T(8,128)(2,1)}, u32[]{:S(2)}) copy-start(bf16[384,512]{1,0:T(8,128)(2,1)} %param.6) | copy-start | bytes 1179652
  6.5 128.7 %reduce-scatter.2.cloned.1.call-start = ((), (), s32[]{:S(2)}) async-start(), calls=%async_computation.1 | async-start | bytes 5160960 | tf_op jit(solution)/shard_map/reduce_scatter | solution.py:56
  7.8 48.4 %collective-permute-start.3 = (bf16[384,512]{0,1:T(8,128)(2,1)S(1)}, bf16[384,512]{0,1:T(8,128)(2,1)}, u32[]{:S(2)}, u32[]{:S(2)}) collective-permute-start(bf16[384,512]{0,1:T(8,128)(2,1)S(1)} %copy.11), channel_id=1, source_target_pairs={{0,8},{4,12},{1,9},{5,13},{2,10},{6,14},{3,11},{7,15},{16,24},{20,... | collective-permute-start | bytes 1179656 | tf_op jit(solution)/shard_map/ppermute | solution.py:17
  9.1 47.1 %collective-permute-start.2 = (bf16[384,512]{0,1:T(8,128)(2,1)S(1)}, bf16[384,512]{0,1:T(8,128)(2,1)}, u32[]{:S(2)}, u32[]{:S(2)}) collective-permute-start(bf16[384,512]{0,1:T(8,128)(2,1)S(1)} %copy.11), channel_id=1, source_target_pairs={{0,4},{4,8},{8,12},{1,5},{5,9},{9,13},{2,6},{6,10},{10,14},{3,7},{... | collective-permute-start | bytes 1179656 | tf_op jit(solution)/shard_map/ppermute | solution.py:17
  12.3 43.1 %collective-permute-start = (bf16[384,512]{1,0:T(8,128)(2,1)}, bf16[384,512]{1,0:T(8,128)(2,1)S(1)}, u32[]{:S(2)}, u32[]{:S(2)}) collective-permute-start(bf16[384,512]{1,0:T(8,128)(2,1)} %param.6), channel_id=1, source_target_pairs={{0,4},{4,8},{8,12},{1,5},{5,9},{9,13},{2,6},{6,10},{10,14},{3,7},{... | collective-permute-start | bytes 1179656 | tf_op jit(solution)/shard_map/ppermute | solution.py:17
  14.2 41.1 %collective-permute-start.1 = (bf16[384,512]{1,0:T(8,128)(2,1)}, bf16[384,512]{1,0:T(8,128)(2,1)S(1)}, u32[]{:S(2)}, u32[]{:S(2)}) collective-permute-start(bf16[384,512]{1,0:T(8,128)(2,1)} %param.6), channel_id=1, source_target_pairs={{0,8},{4,12},{1,9},{5,13},{2,10},{6,14},{3,11},{7,15},{16,24},{20,... | collective-permute-start | bytes 1179656 | tf_op jit(solution)/shard_map/ppermute | solution.py:17
  20.0 37.4 %copy-start = (bf16[384,4,2,128]{3,2,1,0:T(2,128)(2,1)}, bf16[384,4,2,128]{3,2,1,0:T(2,128)(2,1)S(1)}, u32[]{:S(2)}) copy-start(bf16[384,4,2,128]{3,2,1,0:T(2,128)(2,1)S(1)} %reshape.16) | copy-start | bytes 2359300
Sparse Core Ops, SparseCore 0:
  81.9 53.2 reduce-scatter.1
where the time goes:
time: 144 us; the launch traced here: 142 us
  waiting for transfers between devices  88.8 us (62%)
  matrix products  24.3 us (17%)
  between operations  13.5 us (9%)
  starting transfers between devices  7.71 us (5%)
  local copies, waits for them, and re-layouts  4.56 us (3%)
  other arithmetic  3.11 us (2%)
    reduce_scatter x1, waiting for transfers between devices, on_device(): lax.psum_scatter(jnp.dot(attended, out_weight, preferred_element_type=jnp...  53.4 us
    ppermute x4, waiting for transfers between devices, shifted_2(): lax.ppermute(value, axis, [(source, source + steps) for source in range(l...  35.4 us
    dot_general x1, matrix products, on_device(): jnp.dot(attended, out_weight, preferred_element_type=jnp.float32)  10.3 us
    dot_general x1, matrix products, on_device(): jnp.einsum('kgts,skd->tkgd', weights, value_head_stack, preferred_element...  7.79 us
    ppermute x4, starting transfers between devices, shifted_2(): lax.ppermute(value, axis, [(source, source + steps) for source in range(l...  7.71 us
    sub x1, matrix products, on_device(): shifted = jnp.exp(masked - row_max)  6.24 us
  transfers between devices with their start and end apart: 5, of which 2 were waited for; matrix products, arithmetic and copies ran while one was open for 4% of the time, Pallas kernels for 0%

commit v1 on v0

v1 whole, which is shorter than its diff:
```python
import functools
import math

import jax
import jax.numpy as jnp
from jax import lax
from jax.experimental import pallas as pl
from jax.experimental.pallas import tpu as pltpu
from jax.sharding import PartitionSpec as P

QUERY_HEADS = 32
KEY_VALUE_HEADS = 16
HEAD_SIZE = 128
GROUP_WIDTH = QUERY_HEADS // KEY_VALUE_HEADS
CORES = 2

score_scale = 168.0 ** (-0.5) * math.log2(math.e)
MASKED = -1e30

MESH = pl.DeviceIdType.MESH


def layer_kernel(
    n_seq, n_head,
    q_hbm, k_hbm, v_hbm, w_hbm, out_hbm,
    q_buf, kv_buf, top, total, mix, attended, w_buf, partial, core_out, core_in,
    chip_out, chip_in, kept, out_buf,
    q_sem, kv_sem, w_sem, z_send, z_recv, core_send, core_recv, chip_send, chip_recv, out_sem,
):
    kv_local, _, rows, _ = kv_buf.shape[1:]
    n_chunk, _, chunk = w_buf.shape
    block = rows // n_head
    n_chip = n_head // CORES
    reaches = [1 << level for level in range(n_seq.bit_length() - 1)]
    hops = [1] + reaches[:-1] if reaches else []
    seq = lax.axis_index("seq")
    head = lax.axis_index("head")
    chip, core = head // CORES, head % CORES
    core_peer = chip * CORES + 1 - core

    def columns(index, width):
        return pl.ds(pl.multiple_of(index * width, 128), width)

    def kv_load(c, which):
        source = (k_hbm, v_hbm)[which]
        return pltpu.make_async_copy(
            source.at[:, columns(c, HEAD_SIZE)], kv_buf.at[0, c, which], kv_sem.at[c, which]
        )

    def q_load(c, g):
        return pltpu.make_async_copy(
            q_hbm.at[:, columns(c * GROUP_WIDTH + g, HEAD_SIZE)], q_buf.at[c, g], q_sem.at[c, g]
        )

    def w_load(j):
        return pltpu.make_async_copy(w_hbm.at[:, columns(j, chunk)], w_buf.at[j], w_sem.at[j])

    def z_copy(level, c):
        hop = hops[level]
        return pltpu.make_async_remote_copy(
            src_ref=kv_buf.at[level, c],
            dst_ref=kv_buf.at[level + 1, c],
            send_sem=z_send.at[level, c],
            recv_sem=z_recv.at[level, c],
            device_id={"seq": lax.rem(seq + hop, n_seq)},
            device_id_type=MESH,
        )

    def z_sends(level):
        needed = reaches[level - 1] if level else 0
        return jnp.logical_and(seq >= needed, seq + hops[level] < n_seq)

    def core_copy(j):
        return pltpu.make_async_remote_copy(
            src_ref=core_out.at[j],
            dst_ref=core_in.at[j],
            send_sem=core_send.at[j],
            recv_sem=core_recv.at[j],
            device_id={"head": core_peer},
            device_id_type=MESH,
        )

    def chip_copy(j, offset):
        return pltpu.make_async_remote_copy(
            src_ref=chip_out.at[j, offset - 1],
            dst_ref=chip_in.at[j, offset - 1],
            send_sem=chip_send.at[j, offset - 1],
            recv_sem=chip_recv.at[j, offset - 1],
            device_id={"head": lax.rem(chip + offset, n_chip) * CORES + core},
            device_id_type=MESH,
        )

    def out_copy(j):
        return pltpu.make_async_copy(
            out_buf.at[j], out_hbm.at[:, columns(j, chunk)], out_sem.at[j]
        )

    def loop(low, high, body):
        def step(i, carry):
            body(i)
            return carry

        lax.fori_loop(low, high, step, 0)

    barrier = pltpu.get_barrier_semaphore()
    expected = jnp.int32(n_chip)
    for distance in sorted(set(hops)):
        later, earlier = seq + distance < n_seq, seq >= distance

        @pl.when(later)
        def _():
            pl.semaphore_signal(
                barrier, inc=1, device_id={"seq": seq + distance}, device_id_type=MESH
            )

        @pl.when(earlier)
        def _():
            pl.semaphore_signal(
                barrier, inc=1, device_id={"seq": seq - distance}, device_id_type=MESH
            )

        expected += later.astype(jnp.int32) + earlier.astype(jnp.int32)
    pl.semaphore_signal(barrier, inc=1, device_id={"head": core_peer}, device_id_type=MESH)
    for offset in range(1, n_chip):
        pl.semaphore_signal(
            barrier,
            inc=1,
            device_id={"head": lax.rem(chip + offset, n_chip) * CORES + core},
            device_id_type=MESH,
        )

    for c in range(kv_local):
        kv_load(c, 0).start()
        kv_load(c, 1).start()
    for c in range(kv_local):
        for g in range(GROUP_WIDTH):
            q_load(c, g).start()
    pl.semaphore_wait(barrier, expected)

    def send_own(c):
        kv_load(c, 0).wait()
        kv_load(c, 1).wait()
        if reaches:
            @pl.when(z_sends(0))
            def _():
                z_copy(0, c).start()

    loop(0, kv_local, send_own)
    for j in range(n_chunk):
        w_load(j).start()

    def scores_of(level, c):
        stacked = q_buf[c].reshape(GROUP_WIDTH * rows, HEAD_SIZE)
        return score_scale * lax.dot_general(
            stacked, kv_buf[level, c, 0], (((1,), (1,)), ((), ())),
            preferred_element_type=jnp.float32,
        )

    def mixed_values(level, c, shifted):
        return jnp.dot(
            shifted.astype(jnp.bfloat16), kv_buf[level, c, 1], preferred_element_type=jnp.float32
        )

    def own_block(c):
        for g in range(GROUP_WIDTH):
            q_load(c, g).wait()
        shape = (GROUP_WIDTH, rows, rows)
        causal = lax.broadcasted_iota(jnp.int32, shape, 1) >= lax.broadcasted_iota(
            jnp.int32, shape, 2
        )
        scores = scores_of(0, c).reshape(shape)
        scores = jnp.where(causal, scores, MASKED).reshape(GROUP_WIDTH * rows, rows)
        row_max = jnp.max(scores, axis=-1, keepdims=True)
        shifted = jnp.exp2(scores - row_max)
        top[c] = row_max
        total[c] = jnp.sum(shifted, axis=-1, keepdims=True)
        mix[c] = mixed_values(0, c, shifted)

    def earlier_block(level, c):
        scores = scores_of(level, c)
        before = top[c]
        row_max = jnp.maximum(before, jnp.max(scores, axis=-1, keepdims=True))
        fade = jnp.exp2(before - row_max)
        shifted = jnp.exp2(scores - row_max)
        top[c] = row_max
        total[c] = total[c] * fade + jnp.sum(shifted, axis=-1, keepdims=True)
        mix[c] = mix[c] * fade + mixed_values(level, c, shifted)

    def finish(c):
        done = (mix[c] / total[c]).astype(jnp.bfloat16)
        for g in range(GROUP_WIDTH):
            attended[:, columns(c * GROUP_WIDTH + g, HEAD_SIZE)] = done[g * rows : (g + 1) * rows]

    loop(0, kv_local, own_block)
    for level, distance in enumerate(reaches, 1):

        def arrived(c):
            @pl.when(seq >= distance)
            def _():
                z_copy(level - 1, c).wait_recv()
                if level < len(reaches):
                    @pl.when(z_sends(level))
                    def _():
                        z_copy(level, c).start()

                earlier_block(level, c)

            if level == len(reaches):
                finish(c)

        loop(0, kv_local, arrived)
    if not reaches:
        loop(0, kv_local, finish)

    def project(j):
        w_load(j).wait()
        slot = lax.rem(j, 2)
        partial[slot] = jnp.dot(attended[...], w_buf[j], preferred_element_type=jnp.float32)
        for x in range(n_chip):
            start = pl.multiple_of((x * CORES + 1 - core) * block, 8)
            core_out[j, x] = partial[slot, pl.ds(start, block), :].astype(jnp.bfloat16)
        core_copy(j).start()

    def exchange(j):
        slot = lax.rem(j, 2)
        core_copy(j).wait_recv()

        def both_cores(x):
            start = pl.multiple_of((x * CORES + core) * block, 8)
            return partial[slot, pl.ds(start, block), :] + core_in[j, x].astype(jnp.float32)

        for offset in range(1, n_chip):
            chip_out[j, offset - 1] = both_cores(lax.rem(chip + offset, n_chip)).astype(
                jnp.bfloat16
            )
            chip_copy(j, offset).start()
        kept[j] = both_cores(chip)

    def collect(j):
        summed = kept[j]
        for offset in range(1, n_chip):
            chip_copy(j, offset).wait_recv()
            summed += chip_in[j, offset - 1].astype(jnp.float32)
        out_buf[j] = summed.astype(jnp.bfloat16)
        out_copy(j).start()

    project(0)

    def step(j):
        project(j)
        exchange(j - 1)

    loop(1, n_chunk, step)
    exchange(n_chunk - 1)
    loop(0, n_chunk, collect)

    def settle(j):
        core_copy(j).wait_send()
        for offset in range(1, n_chip):
            chip_copy(j, offset).wait_send()
        out_copy(j).wait()

    loop(0, n_chunk, settle)
    for level in range(len(reaches)):

        @pl.when(z_sends(level))
        def _():
            loop(0, kv_local, lambda c: z_copy(level, c).wait_send())


def solution(mesh):
    n_seq, n_head = mesh.shape["seq"], mesh.shape["head"]

    def on_device(queries, keys, values, out_weight):
        rows = queries.shape[0]
        depth, width = out_weight.shape
        kv_local = keys.shape[1] // HEAD_SIZE
        block = rows // n_head
        n_chip = n_head // CORES
        levels = n_seq.bit_length() - 1
        chunk = max(c for c in range(128, 769, 128) if width % c == 0)
        n_chunk = width // chunk
        stacked = GROUP_WIDTH * rows
        bf16, f32, dma = jnp.bfloat16, jnp.float32, pltpu.SemaphoreType.DMA
        anywhere = pl.BlockSpec(memory_space=pl.ANY)
        others = max(1, n_chip - 1)
        return pl.pallas_call(
            functools.partial(layer_kernel, n_seq, n_head),
            out_shape=jax.ShapeDtypeStruct((block, width), bf16),
            in_specs=[anywhere] * 4,
            out_specs=anywhere,
            scratch_shapes=[
                pltpu.VMEM((kv_local, GROUP_WIDTH, rows, HEAD_SIZE), bf16),
                pltpu.VMEM((levels + 1, kv_local, 2, rows, HEAD_SIZE), bf16),
                pltpu.VMEM((kv_local, stacked, 1), f32),
                pltpu.VMEM((kv_local, stacked, 1), f32),
                pltpu.VMEM((kv_local, stacked, HEAD_SIZE), f32),
                pltpu.VMEM((rows, depth), bf16),
                pltpu.VMEM((n_chunk, depth, chunk), bf16),
                pltpu.VMEM((2, rows, chunk), f32),
                pltpu.VMEM((n_chunk, n_chip, block, chunk), bf16),
                pltpu.VMEM((n_chunk, n_chip, block, chunk), bf16),
                pltpu.VMEM((n_chunk, others, block, chunk), bf16),
                pltpu.VMEM((n_chunk, others, block, chunk), bf16),
                pltpu.VMEM((n_chunk, block, chunk), f32),
                pltpu.VMEM((n_chunk, block, chunk), bf16),
                dma((kv_local, GROUP_WIDTH)),
                dma((kv_local, 2)),
                dma((n_chunk,)),
                dma((max(1, levels), kv_local)),
                dma((max(1, levels), kv_local)),
                dma((n_chunk,)),
                dma((n_chunk,)),
                dma((n_chunk, others)),
                dma((n_chunk, others)),
                dma((n_chunk,)),
            ],
            compiler_params=pltpu.CompilerParams(
                collective_id=0, has_side_effects=True, vmem_limit_bytes=48 * 1024 * 1024
            ),
            cost_estimate=pl.CostEstimate(
                flops=2 * rows * depth * width + 4 * rows * rows * (levels + 1) * depth,
                bytes_accessed=2 * depth * width,
                transcendentals=rows * rows * (levels + 1) * depth // HEAD_SIZE,
            ),
        )(queries, keys, values, out_weight)

    in_specs = (
        P(("grp", "seq"), "head"),
        P(("grp", "seq"), "head"),
        P(("grp", "seq"), "head"),
        P("head", None),
    )
    out_specs = P(("grp", "seq", "head"), None)
    return jax.shard_map(
        on_device, mesh=mesh, in_specs=in_specs, out_specs=out_specs, check_vma=False
    )
```

time: 144 us -> 70.4 us (0.49); the launches traced: 142 us -> 70.2 us
  waiting for transfers between devices: 88.8 us -> 0 us
  Pallas kernels: 0 us -> 66.1 us
  matrix products: 24.3 us -> 0 us
  between operations: 13.5 us -> 0.01 us
  starting transfers between devices: 7.71 us -> 0 us
  other arithmetic: 3.11 us -> 0 us
    pallas_call x0 -> x1, Pallas kernels: none -> 66.1 us  [on_device(): pl.pallas_call(functools.partial(layer_kernel, n_seq, n_head), out_shape=...]
    reduce_scatter x1 -> x0, waiting for transfers between devices: 53.4 us -> none  [on_device(): lax.psum_scatter(jnp.dot(attended, out_weight, preferred_element_type=jnp...]
    ppermute x4 -> x0, waiting for transfers between devices: 35.4 us -> none  [shifted_2(): lax.ppermute(value, axis, [(source, source + steps) for source in range(l...]
    dot_general x2 -> x0, matrix products: 18.1 us -> none  [the longest x1 10.3 us: on_device(): jnp.dot(attended, out_weight, preferred_element_type=jnp.float32)]
    ppermute x4 -> x0, starting transfers between devices: 7.71 us -> none  [shifted_2(): lax.ppermute(value, axis, [(source, source + steps) for source in range(l...]
    sub x1 -> x0, matrix products: 6.24 us -> none  [on_device(): shifted = jnp.exp(masked - row_max)]
    concatenate x3 -> x0, other arithmetic: 3.07 us -> none  [the longest x1 1.77 us: on_device(): visible = jnp.concatenate(mask_parts, axis=1)]
    unnamed x5 -> x7, local copies, waits for them, and re-layouts: 1.27 us -> 4.09 us
  transfers between devices with their start and end apart: 5 -> 0, of which waited for: 2 -> 0; matrix products, arithmetic and copies ran while one was open for 4% -> 0% of each run, Pallas kernels for 0% -> 0%
where the time goes in v1:
time: 70.4 us; the launch traced here: 70.2 us
  Pallas kernels  66.1 us (94%)
  local copies, waits for them, and re-layouts  4.09 us (6%)
    pallas_call x1, Pallas kernels, on_device(): pl.pallas_call(functools.partial(layer_kernel, n_seq, n_head), out_shape=...  66.1 us
    unnamed x7, local copies, waits for them, and re-layouts  4.09 us

profile of v1, /device:TPU:21, one launch (start us, length us, event | category | flops | bytes accessed | tf_op | source)
XLA Modules:
  0.0 70.2 jit_solution(15462013519409079759)
XLA Ops:
  0.0 0.0 copy-start
  0.0 1.1 %copy-done = bf16[384,1024]{1,0:T(8,128)(2,1)S(1)} copy-done((bf16[384,1024]{1,0:T(8,128)(2,1)S(1)}, bf16[384,1024]{1,0:T(8,128)(2,1)}, u32[]{:S(2)}) %copy-start) | copy-done | bytes 786456
  1.1 0.0 copy-start.1
  1.1 1.0 %copy-done.1 = bf16[384,512]{1,0:T(8,128)(2,1)S(1)} copy-done((bf16[384,512]{1,0:T(8,128)(2,1)S(1)}, bf16[384,512]{1,0:T(8,128)(2,1)}, u32[]{:S(2)}) %copy-start.1) | copy-done | bytes 393240
  2.1 0.0 copy-start.2
  2.1 1.0 %copy-done.2 = bf16[384,512]{1,0:T(8,128)(2,1)S(1)} copy-done((bf16[384,512]{1,0:T(8,128)(2,1)S(1)}, bf16[384,512]{1,0:T(8,128)(2,1)}, u32[]{:S(2)}) %copy-start.2) | copy-done | bytes 393240
  3.1 66.1 %shard_map.46 = bf16[96,5376]{1,0:T(8,128)(2,1)S(1)} custom-call(bf16[384,1024]{1,0:T(8,128)(2,1)S(1)} %copy-done, bf16[384,512]{1,0:T(8,128)(2,1)S(1)} %copy-done.1, bf16[384,512]{1,0:T(8,128)(2,1)S(1)} %copy-done.2, bf16[1024,5376]{1,0:T(8,128)(2,1)} %w_hbm.1), custom_call_target="tpu_custom_call" | custom-call | flops 6039797760 | bytes 11010048 | tf_op jit(solution)/shard_map/pallas_call | solution.py:287
  69.2 1.0 %copy.6 = bf16[96,5376]{1,0:T(8,128)(2,1)} copy(bf16[96,5376]{1,0:T(8,128)(2,1)S(1)} %shard_map.46) | data formatting | bytes 2064384
Async XLA Ops:
  0.0 1.1 %copy-start = (bf16[384,1024]{1,0:T(8,128)(2,1)S(1)}, bf16[384,1024]{1,0:T(8,128)(2,1)}, u32[]{:S(2)}) copy-start(bf16[384,1024]{1,0:T(8,128)(2,1)} %q_hbm.1) | copy-start | bytes 2359300
  1.1 1.0 %copy-start.1 = (bf16[384,512]{1,0:T(8,128)(2,1)S(1)}, bf16[384,512]{1,0:T(8,128)(2,1)}, u32[]{:S(2)}) copy-start(bf16[384,512]{1,0:T(8,128)(2,1)} %k_hbm.1) | copy-start | bytes 1179652
  2.1 1.0 %copy-start.2 = (bf16[384,512]{1,0:T(8,128)(2,1)S(1)}, bf16[384,512]{1,0:T(8,128)(2,1)}, u32[]{:S(2)}) copy-start(bf16[384,512]{1,0:T(8,128)(2,1)} %v_hbm.1) | copy-start | bytes 1179652

commit v2 on v1

v2 whole, which is shorter than its diff:
```python
import functools
import math

import jax
import jax.numpy as jnp
from jax import lax
from jax.experimental import pallas as pl
from jax.experimental.pallas import tpu as pltpu
from jax.sharding import PartitionSpec as P

QUERY_HEADS = 32
KEY_VALUE_HEADS = 16
HEAD_SIZE = 128
GROUP_WIDTH = QUERY_HEADS // KEY_VALUE_HEADS
CORES = 2
SUB_ROWS = (32, 48, 16)
MOST_COLUMNS = 1792

score_scale = 168.0 ** (-0.5) * math.log2(math.e)
MASKED = -1e30

MESH = pl.DeviceIdType.MESH


def layer_kernel(
    n_seq, n_head,
    q_hbm, k_hbm, v_hbm, w_hbm, out_hbm,
    q_buf, q_in, kv_buf, top, total, mix, attended, w_buf, partial, core_out, core_in,
    chip_out, chip_in, kept, out_buf, o_out, o_in, stat, stat_out, stat_in,
    q_sem, kv_sem, w_sem, z_send, z_recv, q_send, q_recv, o_send, o_recv, stat_send, stat_recv,
    core_send, core_recv, chip_send, chip_recv, out_sem,
):
    kv_local, _, rows, _ = kv_buf.shape[1:]
    n_col, _, chunk = w_buf.shape
    n_part, part_rows = attended.shape[:2]
    sub = part_rows // n_head
    n_step = n_part * n_col
    n_chip = n_head // CORES
    reaches = [1 << level for level in range(n_seq.bit_length() - 1)]
    hops = [1] + reaches[:-1] if reaches else []
    last = len(reaches) - 1
    seq = lax.axis_index("seq")
    head = lax.axis_index("head")
    chip, core = head // CORES, head % CORES
    core_peer = chip * CORES + 1 - core

    def columns(index, width):
        return pl.ds(pl.multiple_of(index * width, 128), width)

    def kv_load(c, which):
        source = (k_hbm, v_hbm)[which]
        return pltpu.make_async_copy(
            source.at[:, columns(c, HEAD_SIZE)], kv_buf.at[0, c, which], kv_sem.at[c, which]
        )

    def q_load(c, g, r):
        return pltpu.make_async_copy(
            q_hbm.at[:, r, :, columns(c * GROUP_WIDTH + g, HEAD_SIZE)],
            q_buf.at[c, g, r],
            q_sem.at[c, g, r],
        )

    def w_load(j):
        return pltpu.make_async_copy(w_hbm.at[:, columns(j, chunk)], w_buf.at[j], w_sem.at[j])

    def later(hop):
        return {"seq": lax.rem(seq + hop, n_seq)}

    def remote(source, target, send, recv, device):
        return pltpu.make_async_remote_copy(
            src_ref=source, dst_ref=target, send_sem=send, recv_sem=recv,
            device_id=device, device_id_type=MESH,
        )

    def z_copy(level, c):
        return remote(
            kv_buf.at[level, c], kv_buf.at[level + 1, c],
            z_send.at[level, c], z_recv.at[level, c], later(hops[level]),
        )

    def z_sends(level):
        needed = reaches[level - 1] if level else 0
        return jnp.logical_and(seq >= needed, seq + hops[level] < n_seq)

    def q_copy(c):
        return remote(
            q_buf.at[c], q_in.at[c], q_send.at[c], q_recv.at[c],
            {"seq": lax.rem(seq + n_seq - hops[last], n_seq)},
        )

    def o_copy(r):
        return remote(o_out.at[r], o_in.at[r], o_send.at[r], o_recv.at[r], later(hops[last]))

    def stat_copy(r):
        return remote(
            stat_out.at[r], stat_in.at[r], stat_send.at[r], stat_recv.at[r], later(hops[last])
        )

    if reaches:
        helped = seq >= reaches[last]
        helps = z_sends(last)

    def core_copy(i):
        return remote(
            core_out.at[i], core_in.at[i], core_send.at[i], core_recv.at[i], {"head": core_peer}
        )

    def chip_copy(i, offset):
        return remote(
            chip_out.at[i, offset - 1], chip_in.at[i, offset - 1],
            chip_send.at[i, offset - 1], chip_recv.at[i, offset - 1],
            {"head": lax.rem(chip + offset, n_chip) * CORES + core},
        )

    def out_copy(i):
        return pltpu.make_async_copy(
            out_buf.at[i], out_hbm.at[i // n_col, :, columns(i % n_col, chunk)], out_sem.at[i]
        )

    def loop(low, high, body):
        def step(i, carry):
            body(i)
            return carry

        lax.fori_loop(low, high, step, 0)

    barrier = pltpu.get_barrier_semaphore()
    expected = jnp.int32(n_chip)

    def greet(device):
        pl.semaphore_signal(barrier, inc=1, device_id=device, device_id_type=MESH)

    for distance in sorted(set(hops)):
        after, before = seq + distance < n_seq, seq >= distance

        @pl.when(after)
        def _():
            greet({"seq": seq + distance})

        @pl.when(before)
        def _():
            greet({"seq": seq - distance})

        expected += after.astype(jnp.int32) + before.astype(jnp.int32)
    greet({"head": core_peer})
    for offset in range(1, n_chip):
        greet({"head": lax.rem(chip + offset, n_chip) * CORES + core})

    def load_head(c):
        kv_load(c, 0).start()
        kv_load(c, 1).start()
        for g in range(GROUP_WIDTH):
            for r in range(n_part):
                q_load(c, g, r).start()

    loop(0, kv_local, load_head)
    pl.semaphore_wait(barrier, expected)

    def send_own(c):
        kv_load(c, 0).wait()
        kv_load(c, 1).wait()
        if last >= 1:
            @pl.when(z_sends(0))
            def _():
                z_copy(0, c).start()

        for g in range(GROUP_WIDTH):
            for r in range(n_part):
                q_load(c, g, r).wait()
        if reaches:
            @pl.when(helped)
            def _():
                q_copy(c).start()

    loop(0, kv_local, send_own)
    loop(0, n_col, lambda j: w_load(j).start())
    stat[...] = jnp.zeros_like(stat)

    stacked = GROUP_WIDTH * rows
    by_part = (GROUP_WIDTH, n_part, part_rows)

    def scores_of(q_ref, level, c):
        return score_scale * lax.dot_general(
            q_ref[c].reshape(stacked, HEAD_SIZE), kv_buf[level, c, 0], (((1,), (1,)), ((), ())),
            preferred_element_type=jnp.float32,
        )

    def mixed_values(level, c, shifted):
        return jnp.dot(
            shifted.astype(jnp.bfloat16), kv_buf[level, c, 1], preferred_element_type=jnp.float32
        ).reshape(by_part + (HEAD_SIZE,))

    def own_block(c):
        shape = (GROUP_WIDTH, n_part, n_head, sub, rows)
        token = (
            lax.broadcasted_iota(jnp.int32, shape, 1) * sub
            + lax.broadcasted_iota(jnp.int32, shape, 2) * (sub * n_part)
            + lax.broadcasted_iota(jnp.int32, shape, 3)
        )
        causal = token >= lax.broadcasted_iota(jnp.int32, shape, 4)
        scores = scores_of(q_buf, 0, c).reshape(shape)
        scores = jnp.where(causal, scores, MASKED).reshape(stacked, rows)
        row_max = jnp.max(scores, axis=-1, keepdims=True)
        shifted = jnp.exp2(scores - row_max)
        top[c] = row_max.reshape(by_part + (1,))
        total[c] = jnp.sum(shifted, axis=-1, keepdims=True).reshape(by_part + (1,))
        mix[c] = mixed_values(0, c, shifted)

    def earlier_block(level, c):
        scores = scores_of(q_buf, level, c)
        before = top[c].reshape(stacked, 1)
        row_max = jnp.maximum(before, jnp.max(scores, axis=-1, keepdims=True))
        fade = jnp.exp2(before - row_max)
        shifted = jnp.exp2(scores - row_max)
        fade = fade.reshape(by_part + (1,))
        top[c] = row_max.reshape(by_part + (1,))
        total[c] = total[c] * fade + jnp.sum(shifted, axis=-1, keepdims=True).reshape(
            by_part + (1,)
        )
        mix[c] = mix[c] * fade + mixed_values(level, c, shifted)

    def help_later(c):
        q_copy(c).wait_recv()
        scores = scores_of(q_in, last, c)
        row_max = jnp.max(scores, axis=-1, keepdims=True)
        shifted = jnp.exp2(scores - row_max)
        row_sum = jnp.sum(shifted, axis=-1, keepdims=True)
        log_sum = (row_max + jnp.log2(row_sum)).reshape(by_part + (1,))
        result = mixed_values(last, c, shifted) / row_sum.reshape(by_part + (1,))
        lane = lax.broadcasted_iota(jnp.int32, stat.shape[1:], 1)
        for g in range(GROUP_WIDTH):
            for r in range(n_part):
                o_out[r, c, g] = result[g, r].astype(jnp.bfloat16)
                stat[r] = jnp.where(lane == c * GROUP_WIDTH + g, log_sum[g, r], stat[r])

    loop(0, kv_local, own_block)
    for level in range(1, last + 1):

        @pl.when(seq >= reaches[level - 1])
        def _():
            def arrived(c):
                z_copy(level - 1, c).wait_recv()
                if level < last:
                    @pl.when(z_sends(level))
                    def _():
                        z_copy(level, c).start()
                else:
                    @pl.when(helps)
                    def _():
                        help_later(c)

                earlier_block(level, c)

            loop(0, kv_local, arrived)

    if reaches:

        @pl.when(helps)
        def _():
            if last == 0:
                loop(0, kv_local, help_later)

            def hand_over(r):
                stat_out[r] = stat[r].T[: stat_out.shape[1]]
                stat_copy(r).start()
                o_copy(r).start()

            loop(0, n_part, hand_over)

    def finish_alone(r):
        for c in range(kv_local):
            for g in range(GROUP_WIDTH):
                h = c * GROUP_WIDTH + g
                attended[r, :, h * HEAD_SIZE : (h + 1) * HEAD_SIZE] = (
                    mix[c, g, r] / total[c, g, r]
                ).astype(jnp.bfloat16)

    def finish_helped(r):
        stat_copy(r).wait_recv()
        o_copy(r).wait_recv()
        log_sums = stat_in[r].T
        for c in range(kv_local):
            for g in range(GROUP_WIDTH):
                h = c * GROUP_WIDTH + g
                log_sum = log_sums[:, h : h + 1]
                row_max = jnp.maximum(top[c, g, r], log_sum)
                here, there = jnp.exp2(top[c, g, r] - row_max), jnp.exp2(log_sum - row_max)
                summed = mix[c, g, r] * here + o_in[r, c, g].astype(jnp.float32) * there
                attended[r, :, h * HEAD_SIZE : (h + 1) * HEAD_SIZE] = (
                    summed / (total[c, g, r] * here + there)
                ).astype(jnp.bfloat16)

    def project(r, j):
        i = r * n_col + j
        slot = lax.rem(i, 2)

        @pl.when(r == 0)
        def _():
            w_load(j).wait()

        partial[slot] = jnp.dot(attended[r], w_buf[j], preferred_element_type=jnp.float32)
        for x in range(n_chip):
            start = pl.multiple_of((x * CORES + 1 - core) * sub, 8)
            core_out[i, x] = partial[slot, pl.ds(start, sub), :].astype(jnp.bfloat16)
        core_copy(i).start()

    def exchange(i):
        slot = lax.rem(i, 2)
        core_copy(i).wait_recv()

        def both_cores(x):
            start = pl.multiple_of((x * CORES + core) * sub, 8)
            return partial[slot, pl.ds(start, sub), :] + core_in[i, x].astype(jnp.float32)

        for offset in range(1, n_chip):
            chip_out[i, offset - 1] = both_cores(lax.rem(chip + offset, n_chip)).astype(
                jnp.bfloat16
            )
            chip_copy(i, offset).start()
        kept[i] = both_cores(chip)

    def collect(i):
        summed = kept[i]
        for offset in range(1, n_chip):
            chip_copy(i, offset).wait_recv()
            summed += chip_in[i, offset - 1].astype(jnp.float32)
        out_buf[i] = summed.astype(jnp.bfloat16)
        out_copy(i).start()

    def row_part(r):
        if reaches:
            @pl.when(helped)
            def _():
                finish_helped(r)

            @pl.when(jnp.logical_not(helped))
            def _():
                finish_alone(r)
        else:
            finish_alone(r)
        project(r, 0)

        def step(j):
            project(r, j)
            exchange(r * n_col + j - 1)

        loop(1, n_col, step)
        exchange(r * n_col + n_col - 1)

    loop(0, n_part, row_part)
    loop(0, n_step, collect)

    def settle(i):
        core_copy(i).wait_send()
        for offset in range(1, n_chip):
            chip_copy(i, offset).wait_send()
        out_copy(i).wait()

    loop(0, n_step, settle)
    for level in range(last):

        @pl.when(z_sends(level))
        def _():
            loop(0, kv_local, lambda c: z_copy(level, c).wait_send())

    if reaches:

        @pl.when(helped)
        def _():
            loop(0, kv_local, lambda c: q_copy(c).wait_send())

        @pl.when(helps)
        def _():
            def sent(r):
                stat_copy(r).wait_send()
                o_copy(r).wait_send()

            loop(0, n_part, sent)


def solution(mesh):
    n_seq, n_head = mesh.shape["seq"], mesh.shape["head"]

    def on_device(queries, keys, values, out_weight):
        rows = queries.shape[0]
        depth, width = out_weight.shape
        kv_local = keys.shape[1] // HEAD_SIZE
        heads = kv_local * GROUP_WIDTH
        block = rows // n_head
        n_chip = n_head // CORES
        levels = max(1, n_seq.bit_length() - 1)
        sub = next((s for s in SUB_ROWS if block % s == 0), block)
        n_part = block // sub
        part_rows = n_head * sub
        chunk = max(c for c in range(128, MOST_COLUMNS + 1, 128) if width % c == 0)
        n_col = width // chunk
        n_step = n_part * n_col
        bf16, f32, dma = jnp.bfloat16, jnp.float32, pltpu.SemaphoreType.DMA
        anywhere = pl.BlockSpec(memory_space=pl.ANY)
        others = max(1, n_chip - 1)
        stat_rows = -(-heads // 8) * 8
        by_part = (kv_local, GROUP_WIDTH, n_part, part_rows)
        result = pl.pallas_call(
            functools.partial(layer_kernel, n_seq, n_head),
            out_shape=jax.ShapeDtypeStruct((n_part, sub, width), bf16),
            in_specs=[anywhere] * 4,
            out_specs=anywhere,
            scratch_shapes=[
                pltpu.VMEM((kv_local, GROUP_WIDTH, n_part, n_head, sub, HEAD_SIZE), bf16),
                pltpu.VMEM((kv_local, GROUP_WIDTH, n_part, n_head, sub, HEAD_SIZE), bf16),
                pltpu.VMEM((levels, kv_local, 2, rows, HEAD_SIZE), bf16),
                pltpu.VMEM(by_part + (1,), f32),
                pltpu.VMEM(by_part + (1,), f32),
                pltpu.VMEM(by_part + (HEAD_SIZE,), f32),
                pltpu.VMEM((n_part, part_rows, depth), bf16),
                pltpu.VMEM((n_col, depth, chunk), bf16),
                pltpu.VMEM((2, part_rows, chunk), f32),
                pltpu.VMEM((n_step, n_chip, sub, chunk), bf16),
                pltpu.VMEM((n_step, n_chip, sub, chunk), bf16),
                pltpu.VMEM((n_step, others, sub, chunk), bf16),
                pltpu.VMEM((n_step, others, sub, chunk), bf16),
                pltpu.VMEM((n_step, sub, chunk), f32),
                pltpu.VMEM((n_step, sub, chunk), bf16),
                pltpu.VMEM((n_part, kv_local, GROUP_WIDTH, part_rows, HEAD_SIZE), bf16),
                pltpu.VMEM((n_part, kv_local, GROUP_WIDTH, part_rows, HEAD_SIZE), bf16),
                pltpu.VMEM((n_part, part_rows, 128), f32),
                pltpu.VMEM((n_part, stat_rows, part_rows), f32),
                pltpu.VMEM((n_part, stat_rows, part_rows), f32),
                dma((kv_local, GROUP_WIDTH, n_part)),
                dma((kv_local, 2)),
                dma((n_col,)),
                dma((levels, kv_local)),
                dma((levels, kv_local)),
                dma((kv_local,)),
                dma((kv_local,)),
                dma((n_part,)),
                dma((n_part,)),
                dma((n_part,)),
                dma((n_part,)),
                dma((n_step,)),
                dma((n_step,)),
                dma((n_step, others)),
                dma((n_step, others)),
                dma((n_step,)),
            ],
            compiler_params=pltpu.CompilerParams(
                collective_id=0, has_side_effects=True, vmem_limit_bytes=60 * 1024 * 1024
            ),
            cost_estimate=pl.CostEstimate(
                flops=2 * rows * depth * width + 4 * rows * rows * (levels + 1) * depth,
                bytes_accessed=2 * depth * width,
                transcendentals=rows * rows * (levels + 1) * depth // HEAD_SIZE,
            ),
        )(queries.reshape(n_head, n_part, sub, -1), keys, values, out_weight)
        return result.reshape(block, width)

    in_specs = (
        P(("grp", "seq"), "head"),
        P(("grp", "seq"), "head"),
        P(("grp", "seq"), "head"),
        P("head", None),
    )
    out_specs = P(("grp", "seq", "head"), None)
    return jax.shard_map(
        on_device, mesh=mesh, in_specs=in_specs, out_specs=out_specs, check_vma=False
    )
```

time: 70.4 us -> 63.6 us (0.903)
  Pallas kernels: 66.1 us -> 61.2 us
  local copies, waits for them, and re-layouts: 4.09 us -> 2.25 us
    pallas_call x1, Pallas kernels: 66.1 us -> 61.2 us  [on_device(): pl.pallas_call(functools.partial(layer_kernel, n_seq, n_head), out_shape=...]
    unnamed x7 -> x1, local copies, waits for them, and re-layouts: 4.09 us -> 2.25 us
where the time goes in v2:
time: 63.6 us; the launch traced here: 63.4 us
  Pallas kernels  61.2 us (96%)
  local copies, waits for them, and re-layouts  2.25 us (4%)
    pallas_call x1, Pallas kernels, on_device(): pl.pallas_call(functools.partial(layer_kernel, n_seq, n_head), out_shape=...  61.2 us
    unnamed x1, local copies, waits for them, and re-layouts  2.25 us

profile of v2, /device:TPU:21, one launch (start us, length us, event | category | flops | bytes accessed | tf_op | source)
XLA Modules:
  0.0 63.4 jit_solution(4911355620994814705)
XLA Ops:
  0.0 61.2 %shard_map.46 = bf16[3,32,5376]{2,1,0:T(8,128)(2,1)} custom-call(bf16[4,3,32,1024]{3,2,1,0:T(8,128)(2,1)} %bitcast.3, bf16[384,512]{1,0:T(8,128)(2,1)} %k_hbm.1, bf16[384,512]{1,0:T(8,128)(2,1)} %v_hbm.1, bf16[1024,5376]{1,0:T(8,128)(2,1)} %w_hbm.1), custom_call_target="tpu_custom_call" | custom-call | flops 6039797760 | bytes 11010048 | tf_op jit(solution)/shard_map/pallas_call | solution.py:403
  61.2 2.2 %copy.6 = bf16[96,5376]{1,0:T(8,128)(2,1)} copy(bf16[96,5376]{1,0:T(8,128)(2,1)} %bitcast.2) | data formatting | bytes 2064384

commit v3 on v2

--- a/solution.py
+++ b/solution.py
@@ -156,23 +156,38 @@
     loop(0, kv_local, load_head)
     pl.semaphore_wait(barrier, expected)
 
-    def send_own(c):
+    def loaded(c):
         kv_load(c, 0).wait()
         kv_load(c, 1).wait()
-        if last >= 1:
-            @pl.when(z_sends(0))
-            def _():
-                z_copy(0, c).start()
-
         for g in range(GROUP_WIDTH):
             for r in range(n_part):
                 q_load(c, g, r).wait()
+
+    def start_own(c):
+        if last >= 1:
+            @pl.when(z_sends(0))
+            def _():
+                z_copy(0, c).start()
+
         if reaches:
             @pl.when(helped)
             def _():
                 q_copy(c).start()
 
-    loop(0, kv_local, send_own)
+    def sent_own(c):
+        if last >= 1:
+            @pl.when(z_sends(0))
+            def _():
+                z_copy(0, c).wait_send()
+
+        if reaches:
+            @pl.when(helped)
+            def _():
+                q_copy(c).wait_send()
+
+    loaded(0)
+    start_own(0)
+    loop(1, kv_local, loaded)
     loop(0, n_col, lambda j: w_load(j).start())
     stat[...] = jnp.zeros_like(stat)
 
@@ -233,39 +248,65 @@
                 o_out[r, c, g] = result[g, r].astype(jnp.bfloat16)
                 stat[r] = jnp.where(lane == c * GROUP_WIDTH + g, log_sum[g, r], stat[r])
 
-    loop(0, kv_local, own_block)
-    for level in range(1, last + 1):
-
+    def hand_over(r):
+        stat_out[r] = stat[r].T[: stat_out.shape[1]]
+        stat_copy(r).start()
+        o_copy(r).start()
+
+    def hand_next(r):
+        if reaches:
+            @pl.when(helps)
+            def _():
+                stat_copy(r).wait_send()
+                o_copy(r).wait_send()
+
+                @pl.when(r + 1 < n_part)
+                def _():
+                    hand_over(r + 1)
+
+    def arrived(level, c):
         @pl.when(seq >= reaches[level - 1])
         def _():
-            def arrived(c):
-                z_copy(level - 1, c).wait_recv()
-                if level < last:
-                    @pl.when(z_sends(level))
+            z_copy(level - 1, c).wait_recv()
+            if level < last:
+                @pl.when(z_sends(level))
+                def _():
+                    z_copy(level, c).start()
+            else:
+                @pl.when(helps)
+                def _():
+                    help_later(c)
+
+                    @pl.when(c == kv_local - 1)
                     def _():
-                        z_copy(level, c).start()
-                else:
-                    @pl.when(helps)
-                    def _():
-                        help_later(c)
-
-                earlier_block(level, c)
-
-            loop(0, kv_local, arrived)
-
-    if reaches:
+                        hand_over(0)
+
+            earlier_block(level, c)
+
+    def first_pass(c):
+        @pl.when(c + 1 < kv_local)
+        def _():
+            own_block(c + 1)
+
+        sent_own(c)
+
+        @pl.when(c + 1 < kv_local)
+        def _():
+            start_own(c + 1)
+
+        if last >= 1:
+            arrived(1, c)
+
+    own_block(0)
+    loop(0, kv_local, first_pass)
+    for level in range(2, last + 1):
+        loop(0, kv_local, functools.partial(arrived, level))
+    if last == 0:
 
         @pl.when(helps)
         def _():
-            if last == 0:
-                loop(0, kv_local, help_later)
-
-            def hand_over(r):
-                stat_out[r] = stat[r].T[: stat_out.shape[1]]
-                stat_copy(r).start()
-                o_copy(r).start()
-
-            loop(0, n_part, hand_over)
+            loop(0, kv_local, help_later)
+            hand_over(0)
 
     def finish_alone(r):
         for c in range(kv_local):
@@ -331,6 +372,7 @@
         if reaches:
             @pl.when(helped)
             def _():
+                hand_next(r)
                 finish_helped(r)
 
             @pl.when(jnp.logical_not(helped))
@@ -346,6 +388,11 @@
 
         loop(1, n_col, step)
         exchange(r * n_col + n_col - 1)
+        if reaches:
+
+            @pl.when(jnp.logical_not(helped))
+            def _():
+                hand_next(r)
 
     loop(0, n_part, row_part)
     loop(0, n_step, collect)
@@ -357,25 +404,11 @@
         out_copy(i).wait()
 
     loop(0, n_step, settle)
-    for level in range(last):
+    for level in range(1, last):
 
         @pl.when(z_sends(level))
         def _():
             loop(0, kv_local, lambda c: z_copy(level, c).wait_send())
-
-    if reaches:
-
-        @pl.when(helped)
-        def _():
-            loop(0, kv_local, lambda c: q_copy(c).wait_send())
-
-        @pl.when(helps)
-        def _():
-            def sent(r):
-                stat_copy(r).wait_send()
-                o_copy(r).wait_send()
-
-            loop(0, n_part, sent)
 
 
 def solution(mesh):

time: 63.6 us -> 61.7 us (0.970); the launches traced: 63.4 us -> 60.7 us
  Pallas kernels: 61.2 us -> 58.4 us
    pallas_call x1, Pallas kernels: 61.2 us -> 58.4 us  [on_device(): pl.pallas_call(functools.partial(layer_kernel, n_seq, n_head), out_shape=...]
where the time goes in v3:
time: 61.7 us; the launch traced here: 60.7 us
  Pallas kernels  58.4 us (95%)
  local copies, waits for them, and re-layouts  2.25 us (4%)
    pallas_call x1, Pallas kernels, on_device(): pl.pallas_call(functools.partial(layer_kernel, n_seq, n_head), out_shape=...  58.4 us
    unnamed x1, local copies, waits for them, and re-layouts  2.25 us

profile of v3, /device:TPU:21, one launch (start us, length us, event | category | flops | bytes accessed | tf_op | source)
XLA Modules:
  0.0 60.7 jit_solution(15651781809162407435)
XLA Ops:
  0.0 58.4 %shard_map.46 = bf16[3,32,5376]{2,1,0:T(8,128)(2,1)} custom-call(bf16[4,3,32,1024]{3,2,1,0:T(8,128)(2,1)} %bitcast.3, bf16[384,512]{1,0:T(8,128)(2,1)} %k_hbm.1, bf16[384,512]{1,0:T(8,128)(2,1)} %v_hbm.1, bf16[1024,5376]{1,0:T(8,128)(2,1)} %w_hbm.1), custom_call_target="tpu_custom_call" | custom-call | flops 6039797760 | bytes 11010048 | tf_op jit(solution)/shard_map/pallas_call | solution.py:436
  58.4 2.2 %copy.6 = bf16[96,5376]{1,0:T(8,128)(2,1)} copy(bf16[96,5376]{1,0:T(8,128)(2,1)} %bitcast.2) | data formatting | bytes 2064384
